TPU v7x, 256 devices: a whole 4x4x8 slice. The times are simulated.
256 devices in a mesh: fsdp: 64 (over y_hi, x, z), tp: 4 (over y_lo, core).
Axes of the slice: x: 4, y: 4 (y_hi: 2, y_lo: 2; y = y_hi * 2 + y_lo), z: 8, core: 2. Of those that a mesh axis runs over, the one named last changes fastest.
Arguments:
- tokens: bfloat16 [8192, 8192], P('fsdp', 'tp'), may hold values from -32 to 32
- gain: bfloat16 [8192], P('tp'), may hold values from 0.25 to 1.75
- w_query: bfloat16 [8192, 512], P('fsdp', 'tp'), may hold values from -0.055242717 to 0.055242717
- w_key: bfloat16 [8192, 128], P('fsdp'), may hold values from -1.2153398 to 1.2153398
- w_value: bfloat16 [8192, 128], P('fsdp'), may hold values from -0.0625 to 0.0625
- w_out: bfloat16 [512, 8192], P('tp', 'fsdp'), may hold values from -0.0625 to 0.0625
- cotangent: bfloat16 [8192, 8192], P('fsdp', 'tp'), may hold values from -6 to 6
Outputs:
- grad_input: float32 [8192, 8192], P('fsdp', 'tp')
- grad_gain: float32 [8192], P('tp')
- grad_query: float32 [8192, 512], P('fsdp', 'tp')
- grad_key: float32 [8192, 128], P('fsdp')
- grad_value: float32 [8192, 128], P('fsdp')
- grad_out: float32 [512, 8192], P('tp', 'fsdp')
All inputs are finite; a program needn't handle non-finite values.
Results may differ from a plain program's by a relative error of at most 0.024.
Values may be sent and summed in bfloat16 or wider, within the bound.
No kernel may reach another device: no remote copies, remote signals or barrier semaphores. Data moves between devices by JAX's collectives and lax.ppermute only.
A program may use at most 128 MiB of HBM per device.

v0:
```python
import math

import jax
import jax.numpy as jnp
from jax import lax
from jax.sharding import PartitionSpec as P

HD = 128


def attend(query, key_rows, value_rows, attn_grad):
    row_count = query.shape[0]
    heads = query.shape[1] // HD
    query_h = query.reshape(row_count, heads, HD)
    grad_h = attn_grad.reshape(row_count, heads, HD)
    scores = jnp.einsum(
        "thd,sd->hts", query_h, key_rows, preferred_element_type=jnp.float32
    ) * HD ** (-0.5)
    causal = jnp.arange(row_count)[:, None] >= jnp.arange(row_count)[None, :]
    scores = jnp.where(causal[None], scores, jnp.float32(-1e30))
    row_peak = jnp.max(scores, axis=-1, keepdims=True)
    shifted = jnp.exp(scores - row_peak)
    softmax_out = shifted / jnp.sum(shifted, axis=-1, keepdims=True)
    rounded = softmax_out.astype(jnp.bfloat16)
    attended = jnp.einsum(
        "hts,sd->thd", rounded, value_rows, preferred_element_type=jnp.float32
    ).astype(jnp.bfloat16)
    dprob = jnp.einsum("thd,sd->hts", grad_h, value_rows, preferred_element_type=jnp.float32)
    dscore = (
        softmax_out * (dprob - jnp.sum(dprob * softmax_out, axis=-1, keepdims=True)) * HD ** (-0.5)
    )
    dscore = dscore.astype(jnp.bfloat16)
    d_query = jnp.einsum(
        "hts,sd->thd", dscore, key_rows, preferred_element_type=jnp.float32
    ).astype(jnp.bfloat16)
    d_key = jnp.einsum("hts,thd->shd", dscore, query_h, preferred_element_type=jnp.float32).astype(
        jnp.bfloat16
    )
    d_value = jnp.einsum(
        "hts,thd->shd", rounded, grad_h, preferred_element_type=jnp.float32
    ).astype(jnp.bfloat16)
    width_all = heads * HD
    return (
        attended.reshape(row_count, width_all),
        d_query.reshape(row_count, width_all),
        d_key.reshape(row_count, width_all),
        d_value.reshape(row_count, width_all),
    )


def local(tokens, gain, w_query, w_key, w_value, w_out, cotangent):
    tok_count = tokens.shape[0]
    quarter = tokens.shape[1]
    group_count = lax.axis_size("fsdp")
    head_width = w_query.shape[1]
    features, gain_all, cot_all = (
        lax.all_gather(tokens, "tp", axis=1, tiled=True),
        lax.all_gather(gain, "tp", axis=0, tiled=True),
        lax.all_gather(cotangent, "tp", axis=1, tiled=True),
    )
    loss_scale = 1.0 / math.sqrt(tok_count * group_count)
    values_f = features.astype(jnp.float32)
    inv_rms = lax.rsqrt(jnp.mean(values_f * values_f, axis=-1, keepdims=True) + 1e-05)
    unit_rows = values_f * inv_rms
    normed = (unit_rows * gain_all.astype(jnp.float32)).astype(jnp.bfloat16)
    stacked = jnp.concatenate(
        (
            lax.all_gather(w_query, "fsdp", axis=0, tiled=True),
            lax.all_gather(w_key, "fsdp", axis=0, tiled=True),
            lax.all_gather(w_value, "fsdp", axis=0, tiled=True),
        ),
        axis=1,
    )
    columns = normed
    total = jnp.dot(columns, stacked, preferred_element_type=jnp.float32)
    query = total[:, :head_width].astype(jnp.bfloat16)
    key_rows = total[:, head_width : 2 * head_width].astype(jnp.bfloat16)
    value_rows = total[:, 2 * head_width :].astype(jnp.bfloat16)
    columns = cot_all
    attn_grad = lax.dot_general(
        columns,
        lax.all_gather(w_out, "fsdp", axis=1, tiled=True),
        (((1,), (1,)), ((), ())),
        preferred_element_type=jnp.float32,
    ).astype(jnp.bfloat16)
    attended, d_query, d_key, d_value = attend(query, key_rows, value_rows, attn_grad)
    head_grads = jnp.concatenate([d_query, d_key, d_value], axis=1)
    partial_sum = lax.dot_general(
        head_grads, stacked, (((1,), (1,)), ((), ())), preferred_element_type=jnp.float32
    )
    partial_sum = lax.optimization_barrier(partial_sum.astype(jnp.bfloat16)).astype(jnp.float32)
    quarter_start = lax.axis_index("tp") * quarter
    summed = lax.psum(partial_sum.astype(jnp.bfloat16), "tp").astype(jnp.float32)
    scaled = summed * gain_all.astype(jnp.float32)
    row_mean = jnp.mean(scaled * unit_rows, axis=-1, keepdims=True)
    full_grad = inv_rms * (scaled - unit_rows * row_mean)
    grad_input = lax.dynamic_slice_in_dim(full_grad, quarter_start, quarter, 1)
    summed_own = lax.dynamic_slice_in_dim(summed, quarter_start, quarter, 1)
    unit_own = lax.dynamic_slice_in_dim(unit_rows, quarter_start, quarter, 1)
    gain_term = jnp.sum(summed_own * unit_own, axis=0)
    grad_gain = lax.psum(gain_term, "fsdp") * loss_scale
    first = lax.dot_general(
        normed, head_grads, (((0,), (0,)), ((), ())), preferred_element_type=jnp.float32
    )
    second = lax.dot_general(
        cot_all, attended, (((0,), (0,)), ((), ())), preferred_element_type=jnp.float32
    )
    summed_grads = lax.psum_scatter(
        jnp.concatenate([first, second], axis=1), "fsdp", scatter_dimension=0, tiled=True
    )
    summed_grads = summed_grads * loss_scale
    grad_query = summed_grads[:, :head_width]
    shared_grads = lax.psum(
        summed_grads[:, head_width : 3 * head_width].astype(jnp.bfloat16), "tp"
    ).astype(jnp.float32)
    grad_key = shared_grads[:, :head_width]
    grad_value = shared_grads[:, head_width:]
    grad_out = summed_grads[:, 3 * head_width :].T
    return (grad_input, grad_gain, grad_query, grad_key, grad_value, grad_out)


def solution(mesh):
    in_specs = (
        P("fsdp", "tp"),
        P("tp"),
        P("fsdp", "tp"),
        P("fsdp", None),
        P("fsdp", None),
        P("tp", "fsdp"),
        P("fsdp", "tp"),
    )
    out_specs = (
        P("fsdp", "tp"),
        P("tp"),
        P("fsdp", "tp"),
        P("fsdp", None),
        P("fsdp", None),
        P("tp", "fsdp"),
    )
    return jax.shard_map(local, mesh=mesh, in_specs=in_specs, out_specs=out_specs, check_vma=False)
```

profile of v0, /device:TPU:8, one launch (start us, length us, event | category | flops | bytes accessed | tf_op | source)
XLA Modules:
  0.0 1212.7 jit_solution(321811103295041013)
XLA Ops:
  7.2 0.7 all-gather.7.cloned.1.call-update
  7.9 0.7 all-gather.9.cloned.1.call-update
  8.7 0.7 all-gather.11.cloned.1.call-update
  11.2 5.6 all_gather.22
  16.7 25.9 %all-gather.7.cloned.1.call-done = bf16[128,8192]{1,0:T(8,128)(2,1)} async-done(((bf16[128,2048]{1,0:T(8,128)(2,1)}), bf16[128,8192]{1,0:T(8,128)(2,1)}) %all-gather.7.cloned.1.call-update) | async-done | bytes 2097168 | tf_op jit(solution)/shard_map/all_gather | solution.py:57
  42.7 2.1 fusion
  44.8 121.1 %all-gather.9.cloned.1.call-done = bf16[8192,128]{1,0:T(8,128)(2,1)} async-done(((bf16[128,128]{1,0:T(8,128)(2,1)}), bf16[8192,128]{1,0:T(8,128)(2,1)}) %all-gather.9.cloned.1.call-update) | async-done | bytes 2097168 | tf_op jit(solution)/shard_map/all_gather | solution.py:68
  165.8 3.1 constant_dynamic-update-slice_fusion.2
  168.9 115.1 %all-gather.11.cloned.1.call-done = bf16[8192,128]{1,0:T(8,128)(2,1)} async-done(((bf16[128,128]{1,0:T(8,128)(2,1)}), bf16[8192,128]{1,0:T(8,128)(2,1)}) %all-gather.11.cloned.1.call-update) | async-done | bytes 2097168 | tf_op jit(solution)/shard_map/all_gather | solution.py:69
  284.0 3.1 constant_dynamic-update-slice_fusion.1
  287.1 114.9 %all-gather.13.cloned.1.call-done = bf16[8192,128]{1,0:T(8,128)(2,1)} async-done(((bf16[128,128]{1,0:T(8,128)(2,1)}), bf16[8192,128]{1,0:T(8,128)(2,1)}) %all-gather.13.cloned.1.call-update) | async-done | bytes 2097168 | tf_op jit(solution)/shard_map/all_gather | solution.py:70
  402.0 3.2 constant_dynamic-update-slice_fusion
  405.2 4.1 convolution_convert_fusion.1
  409.5 21.7 %all-gather.15.cloned.1.call-done = bf16[128,8192]{1,0:T(8,128)(2,1)} async-done(((bf16[128,2048]{1,0:T(8,128)(2,1)}), bf16[128,8192]{1,0:T(8,128)(2,1)}) %all-gather.15.cloned.1.call-update) | async-done | bytes 2097168 | tf_op jit(solution)/shard_map/all_gather | solution.py:59
  431.2 105.3 %all-gather.17.cloned.1.call-done = bf16[128,8192]{1,0:T(8,128)(2,1)} async-done(((bf16[128,128]{1,0:T(8,128)(2,1)}), bf16[128,8192]{1,0:T(8,128)(2,1)}) %all-gather.17.cloned.1.call-update) | async-done | bytes 2097168 | tf_op jit(solution)/shard_map/all_gather | solution.py:82
  536.5 2.9 convolution_convert_fusion.6
  540.2 4.4 convolution_bitcast_fusion
  544.7 1.9 fusion.8
  546.8 6.0 pad_maximum_fusion
  552.9 6.2 convolution_convert_fusion
  559.1 393.4 %reduce-scatter.2.cloned.1.call-done = f32[128,512]{0,1:T(8,128)} async-done(((f32[8192,512]{0,1:T(8,128)}), f32[128,512]{0,1:T(8,128)}) %reduce-scatter.2.cloned.1.call-update) | async-done | bytes 262160 | tf_op jit(solution)/shard_map/reduce_scatter | solution.py:108
  952.5 1.0 broadcast_multiply_fusion.1
  953.4 0.6 slice.59
  954.1 0.6 slice_bitcast_fusion
  954.7 0.7 copy.16
  955.5 56.8 %all-reduce.3.cloned.1.call-done = (bf16[128,256]{0,1:T(8,128)(2,1)}, bf16[128,8192]{1,0:T(8,128)(2,1)}) async-done(((bf16[128,256]{0,1:T(8,128)(2,1)}, bf16[128,8192]{1,0:T(8,128)(2,1)}), (bf16[128,256]{0,1:T(8,128)(2,1)}, bf16[128,8192]{1,0:T(8,128)(2,1)})) %all-reduce.3.cloned.1.call-update) | async-done | bytes 2162704 | tf_op jit(solution)/shard_map/psum | solution.py:113
  1012.3 2.2 convert_element_type.86
  1014.5 1.7 multiply_reduce_fusion
  1016.2 1.3 multiply_reduce_fusion.1
  1017.5 186.3 %psum.22 = f32[2048]{0:T(1024)S(1)} all-reduce(f32[2048]{0:T(1024)S(1)} %get-tuple-element.20), channel_id=1, replica_groups=mesh['fsdp'=64,'tp'=4] {'fsdp'}, use_global_device_ids=true, to_apply=%region_7.8 | all-reduce | flops 2048 | bytes 16384 | tf_op jit(solution)/shard_map/psum | solution.py:101
  1204.4 0.7 copy.17
  1205.2 0.7 copy.18
  (33 shorter events, 3.9 us)
Async XLA Ops:
  7.2 35.5 %all-gather.7.cloned.1.call-start = ((), (), s32[]{:S(2)}) async-start(), calls=%async_computation.1 | async-start | bytes 2621440 | tf_op jit(solution)/shard_map/all_gather | solution.py:57
  7.9 157.9 %all-gather.9.cloned.1.call-start = ((), (), s32[]{:S(2)}) async-start(), calls=%async_computation.2 | async-start | bytes 2129920 | tf_op jit(solution)/shard_map/all_gather | solution.py:68
  8.6 275.3 %all-gather.11.cloned.1.call-start = ((), (), s32[]{:S(2)}) async-start(), calls=%async_computation.3 | async-start | bytes 2129920 | tf_op jit(solution)/shard_map/all_gather | solution.py:69
  9.4 392.6 %all-gather.13.cloned.1.call-start = ((), (), s32[]{:S(2)}) async-start(), calls=%async_computation.4 | async-start | bytes 2129920 | tf_op jit(solution)/shard_map/all_gather | solution.py:70
  10.0 421.3 %all-gather.15.cloned.1.call-start = ((), (), s32[]{:S(2)}) async-start(), calls=%async_computation.5 | async-start | bytes 2621440 | tf_op jit(solution)/shard_map/all_gather | solution.py:59
  10.5 526.0 %all-gather.17.cloned.1.call-start = ((), (), s32[]{:S(2)}) async-start(), calls=%async_computation.6 | async-start | bytes 2129920 | tf_op jit(solution)/shard_map/all_gather | solution.py:82
  11.1 941.3 %reduce-scatter.2.cloned.1.call-start = ((), (), s32[]{:S(2)}) async-start(), calls=%async_computation.7 | async-start | bytes 17039360 | tf_op jit(solution)/shard_map/reduce_scatter | solution.py:108
  168.9 236.3 %copy-start = (bf16[128,8192]{1,0:T(8,128)(2,1)S(1)}, bf16[128,8192]{1,0:T(8,128)(2,1)}, u32[]{:S(2)}) copy-start(bf16[128,8192]{1,0:T(8,128)(2,1)} %all-gather.7.cloned.1.call-done) | copy-start | bytes 6291460
  544.6 2.2 copy-start.1
  552.8 459.5 %all-reduce.3.cloned.1.call-start = ((), (), s32[]{:S(2)}) async-start(), calls=%async_computation.8 | async-start | bytes 4325376 | tf_op jit(solution)/shard_map/psum | solution.py:113
  1012.3 2.2 copy-start.2
  1016.2 188.3 %copy-start.3 = (bf16[128,256]{0,1:T(8,128)(2,1)S(1)}, bf16[128,256]{0,1:T(8,128)(2,1)}, u32[]{:S(2)}) copy-start(bf16[128,256]{0,1:T(8,128)(2,1)} %get-tuple-element.18) | copy-start | bytes 196612
Sparse Core Ops, SparseCore 0:
  9.8 32.8 all-gather.6
  46.4 119.3 all-gather.8
  169.6 114.3 all-gather.10
  287.6 114.3 all-gather.12
  403.6 27.5 all-gather.14
  434.5 101.9 all-gather.16
  552.9 399.4 reduce-scatter.1
  955.8 56.4 all-reduce.2
where the time goes:
time: 1210 us
  waiting for transfers between devices  958 us (79%)
  blocking collectives  192 us (16%)
  matrix products  20.4 us (2%)
  other arithmetic  14.8 us (1%)
  between operations  14.2 us (1%)
  local copies, waits for them, and re-layouts  13.3 us (1%)
    reduce_scatter x1, waiting for transfers between devices, local(): lax.psum_scatter(jnp.concatenate([first, second], axis=1), 'fsdp', scatte...  393 us
    psum x1, blocking collectives, local(): grad_gain = lax.psum(gain_term, 'fsdp') * loss_scale  186 us
    all_gather x1, waiting for transfers between devices, local(): lax.all_gather(w_query, 'fsdp', axis=0, tiled=True)  121 us
    all_gather x1, waiting for transfers between devices, local(): lax.all_gather(w_key, 'fsdp', axis=0, tiled=True)  115 us
    all_gather x1, waiting for transfers between devices, local(): lax.all_gather(w_value, 'fsdp', axis=0, tiled=True)  115 us
    all_gather x1, waiting for transfers between devices, local(): lax.all_gather(w_out, 'fsdp', axis=1, tiled=True)  105 us
    psum x1, waiting for transfers between devices, local(): lax.psum(summed_grads[:, head_width:3 * head_width].astype(jnp.bfloat16),...  56.8 us
    all_gather x1, waiting for transfers between devices, local(): lax.all_gather(tokens, 'tp', axis=1, tiled=True)  25.9 us
  transfers between devices with their start and end apart: 8, of which 8 were waited for; matrix products, arithmetic and copies ran while one was open for 2% of the time, Pallas kernels for 0%

commit v1 on v0

v1 whole, which is shorter than its diff:
```python
import math

import jax
import jax.numpy as jnp
from jax import lax
from jax.sharding import Mesh, PartitionSpec as P

HD = 128
NX = 4
NZ = 8
AXES = ("yh", "x", "z", "yl", "c")
FSDP = ("yh", "x", "z")
TP = ("yl", "c")
F32 = jnp.float32
BF16 = jnp.bfloat16


def flat(yh, x, z, yl, c):
    return (((yh * NX + x) * NZ + z) * 2 + yl) * 2 + c


def owner_perm(flip):
    pairs = []
    for yh in range(2):
        for x in range(NX):
            for z in range(NZ):
                for yl in range(2):
                    for c in range(2):
                        dest_x = (x % 2) * 2 + z // 4
                        dest_z = c * 4 + z % 4
                        pairs.append((flat(yh, x, z, yl, c), flat(yl ^ flip, dest_x, dest_z, yh, x // 2)))
    return pairs


def inverse(pairs):
    return [(d, s) for s, d in pairs]


def shift_x(value, by):
    return lax.ppermute(value, "x", [(i, (i + by) % NX) for i in range(NX)])


def swap(value, axis):
    return lax.ppermute(value, axis, [(0, 1), (1, 0)])


def dot(a, b, ca, cb):
    return lax.dot_general(a, b, (((ca,), (cb,)), ((), ())), preferred_element_type=F32)


def attend(query, key_rows, value_rows, attn_grad):
    rows = query.shape[0]
    scores = dot(query, key_rows, 1, 1) * HD ** (-0.5)
    causal = jnp.arange(rows)[:, None] >= jnp.arange(rows)[None, :]
    scores = jnp.where(causal, scores, jnp.float32(-1e30))
    peak = jnp.max(scores, axis=-1, keepdims=True)
    shifted = jnp.exp(scores - peak)
    softmax_out = shifted / jnp.sum(shifted, axis=-1, keepdims=True)
    rounded = softmax_out.astype(BF16)
    attended = dot(rounded, value_rows, 1, 0).astype(BF16)
    dprob = dot(attn_grad, value_rows, 1, 1)
    dscore = softmax_out * (dprob - jnp.sum(dprob * softmax_out, axis=-1, keepdims=True)) * HD ** (-0.5)
    dscore = dscore.astype(BF16)
    d_query = dot(dscore, key_rows, 1, 0).astype(BF16)
    d_key = dot(dscore, query, 0, 0)
    d_value = dot(rounded, attn_grad, 0, 0)
    return attended, d_query, d_key.astype(BF16), d_value.astype(BF16)


def local(tokens, gain, w_query, w_key, w_value, w_out, cotangent):
    rows, quarter = tokens.shape
    sub = quarter // NX
    width = quarter * 4
    yh, x, yl, c = (lax.axis_index(a) for a in ("yh", "x", "yl", "c"))
    head = yl * 2 + c
    loss_scale = 1.0 / math.sqrt(rows * 64)

    piece = rows // 4
    pack = jnp.concatenate(
        [
            w_query,
            w_out,
            lax.dynamic_slice_in_dim(w_key, head * piece, piece, 0),
            lax.dynamic_slice_in_dim(w_value, head * piece, piece, 0),
        ],
        axis=0,
    )
    same = lax.ppermute(pack, AXES, owner_perm(0))
    other = lax.ppermute(pack, AXES, owner_perm(1))
    first = jnp.where(yh == 0, same, other)
    second = jnp.where(yh == 0, other, same)
    both = jnp.stack([first, second])
    gathered = lax.all_gather(both, "z")
    gathered = gathered.reshape(2, 4, 2, *pack.shape)

    values_f = tokens.astype(F32)
    square_sum = jnp.sum(values_f * values_f, axis=-1, keepdims=True)
    inv_rms = lax.rsqrt(lax.psum(square_sum, TP) / width + 1e-05)
    unit_rows = values_f * inv_rms
    gain_f = gain.astype(F32)
    normed = (unit_rows * gain_f).astype(BF16)

    def spread(value):
        parts = [lax.dynamic_slice_in_dim(value, ((x + s) % NX) * sub, sub, 1) for s in range(NX)]
        return jnp.concatenate([parts[0]] + [shift_x(parts[s], s) for s in range(1, NX)], axis=0)

    cot_sw = spread(cotangent)
    normed_sw = spread(normed)

    def columns(side):
        block = gathered[side]
        w_q = jnp.transpose(block[:, :, :HD], (0, 2, 1, 3)).reshape(sub, 2 * HD)
        w_o = jnp.transpose(block[:, :, HD : 2 * HD], (1, 2, 0, 3)).reshape(2 * HD, sub)
        return w_q, w_o

    def shared(start):
        block = gathered[:, :, :, start : start + piece]
        return jnp.transpose(block, (1, 2, 0, 3, 4)).reshape(sub, HD)

    w_k, w_v = shared(2 * HD), shared(2 * HD + piece)
    w_mine = jnp.where(c == 0, w_k, w_v)
    w_theirs = jnp.where(c == 0, w_v, w_k)

    def partial(side, w_shared):
        w_q, w_o = columns(side)
        left = dot(normed_sw, jnp.concatenate([w_q, w_shared], axis=1), 1, 0)
        return jnp.concatenate([left, dot(cot_sw, w_o, 1, 1)], axis=1)

    theirs = partial(1 - c, w_theirs)
    mine = partial(c, w_mine)
    total = mine + swap(theirs, "c")
    total = total.reshape(NX, rows, 5 * HD)
    own = total[0]
    for s in range(1, NX):
        own = own + shift_x(total[s], -s)
    q01, kv, a01 = own[:, : 2 * HD], own[:, 2 * HD : 3 * HD], own[:, 3 * HD :]
    keep = jnp.where(yl == 0, jnp.concatenate([q01[:, :HD], a01[:, :HD]], 1), jnp.concatenate([q01[:, HD:], a01[:, HD:]], 1))
    give = jnp.where(yl == 0, jnp.concatenate([q01[:, HD:], a01[:, HD:]], 1), jnp.concatenate([q01[:, :HD], a01[:, :HD]], 1))
    got = swap(jnp.concatenate([give, kv], 1), "yl")
    final = (jnp.concatenate([keep, kv], 1) + got).astype(BF16)
    query, attn_grad, kv_mine = final[:, :HD], final[:, HD : 2 * HD], final[:, 2 * HD :]
    kv_theirs = swap(kv_mine, "c")
    key_rows = jnp.where(c == 0, kv_mine, kv_theirs)
    value_rows = jnp.where(c == 0, kv_theirs, kv_mine)

    attended, d_query, d_key, d_value = attend(query, key_rows, value_rows, attn_grad)

    sum_mine = jnp.where(c == 0, d_key, d_value).astype(F32)
    sum_mine = (sum_mine + swap(jnp.where(c == 0, d_value, d_key), "c").astype(F32)).astype(BF16)
    heads_own = jnp.concatenate([d_query, attended, sum_mine], axis=1)
    heads_x = jnp.concatenate([heads_own] + [shift_x(heads_own, s) for s in range(1, NX)], axis=0)
    heads_yl = swap(heads_x, "yl")
    lower = jnp.where(yl == 0, heads_x, heads_yl)
    upper = jnp.where(yl == 0, heads_yl, heads_x)
    shared_sum = (heads_x[:, 2 * HD :].astype(F32) + heads_yl[:, 2 * HD :].astype(F32)).astype(BF16)
    side_mine = jnp.concatenate([lower[:, :HD], upper[:, :HD], lower[:, HD : 2 * HD], upper[:, HD : 2 * HD], shared_sum], 1)
    side_theirs = swap(side_mine, "c")
    even = jnp.where(c == 0, side_mine, side_theirs)
    odd = jnp.where(c == 0, side_theirs, side_mine)
    d_heads = jnp.concatenate([even[:, : 2 * HD], odd[:, : 2 * HD], even[:, 4 * HD :], odd[:, 4 * HD :]], 1)
    attended_all = jnp.concatenate([even[:, 2 * HD : 4 * HD], odd[:, 2 * HD : 4 * HD]], 1)

    grads = dot(normed_sw, d_heads, 0, 0).astype(BF16)
    grad_o = dot(attended_all, cot_sw, 0, 0).astype(BF16)
    g_q = grads[:, : 4 * HD].reshape(4, HD, 2, 2, HD).transpose(2, 0, 3, 1, 4)
    g_o = grad_o.reshape(2, 2, HD, 4, HD).transpose(0, 3, 1, 2, 4)
    g_k = grads[:, 4 * HD : 5 * HD].reshape(4, 2, 2, piece, HD).transpose(2, 0, 1, 3, 4)
    g_v = grads[:, 5 * HD :].reshape(4, 2, 2, piece, HD).transpose(2, 0, 1, 3, 4)
    terms = jnp.concatenate([g_q, g_o, g_k, g_v], axis=3).reshape(NZ, 2, 2 * HD + 2 * piece, HD)
    scattered = lax.psum_scatter(terms, "z", scatter_dimension=0)
    to_same = jnp.where(yh == 0, scattered[0], scattered[1])
    to_other = jnp.where(yh == 0, scattered[1], scattered[0])
    summed_grads = lax.ppermute(to_same, AXES, inverse(owner_perm(0))).astype(F32)
    summed_grads = (summed_grads + lax.ppermute(to_other, AXES, inverse(owner_perm(1))).astype(F32)) * loss_scale
    grad_query = summed_grads[:HD]
    grad_out = summed_grads[HD : 2 * HD]
    shared_grads = lax.all_gather(summed_grads[2 * HD :].reshape(2, piece, HD), TP)
    grad_key = shared_grads[:, 0].reshape(rows, HD)
    grad_value = shared_grads[:, 1].reshape(rows, HD)

    w_even, o_even = columns(0)
    w_odd, o_odd = columns(1)
    w_all = jnp.concatenate([w_even, w_odd, w_k, w_v], axis=1)
    back = dot(d_heads, w_all, 1, 1).astype(BF16).reshape(NX, rows, sub)
    pieces = [back[0]] + [shift_x(back[s], -s) for s in range(1, NX)]
    summed = jnp.zeros((rows, quarter), BF16)
    for s in range(NX):
        summed = lax.dynamic_update_slice_in_dim(summed, pieces[s], ((x + s) % NX) * sub, 1)
    summed = summed.astype(F32)
    scaled = summed * gain_f
    row_mean = lax.psum(jnp.sum(scaled * unit_rows, axis=-1, keepdims=True), TP) / width
    grad_input = inv_rms * (scaled - unit_rows * row_mean)
    gain_term = jnp.sum(summed * unit_rows, axis=0)
    gain_terms = lax.all_to_all(jnp.broadcast_to(gain_term.reshape(1, 16, 128), (64, 16, 128)), FSDP, 0, 0)
    grad_gain = jnp.sum(gain_terms, axis=0).reshape(quarter) * loss_scale
    return (grad_input, grad_gain, grad_query, grad_key, grad_value, grad_out)


def solution(mesh):
    fine = Mesh(mesh.devices.reshape(2, NX, NZ, 2, 2), AXES)
    in_specs = (P(FSDP, TP), P(TP), P(FSDP, TP), P(FSDP, None), P(FSDP, None), P(TP, FSDP), P(FSDP, TP))
    out_specs = (P(FSDP, TP), P(TP), P(FSDP, TP), P(FSDP, None), P(FSDP, None), P(TP, FSDP))
    return jax.shard_map(local, mesh=fine, in_specs=in_specs, out_specs=out_specs, check_vma=False)
```

time: 1210 us -> 225 us (0.19)
  waiting for transfers between devices: 958 us -> 100 us
  blocking collectives: 192 us -> 27.3 us
  starting transfers between devices: 0.31 us -> 44.1 us
  matrix products: 20.4 us -> 4.18 us
    all_gather x6 -> x1, waiting for transfers between devices: 504 us -> 20.7 us  [local(): gathered = lax.all_gather(both, 'z')]
    reduce_scatter x1, waiting for transfers between devices: 393 us -> 0.02 us  [local(): scattered = lax.psum_scatter(terms, 'z', scatter_dimension=0)]
    psum x1 -> x2, blocking collectives: 186 us -> 18.3 us  [the longest x1 11.9 us: local(): inv_rms = lax.rsqrt(lax.psum(square_sum, TP) / width + 1e-05)]
    ppermute x0 -> x25, waiting for transfers between devices: none -> 64 us  [the longest x15 34 us: shift_x(): return lax.ppermute(value, 'x', [(i, (i + by) % NX) for i in range(NX)])]
    psum x1 -> x0, waiting for transfers between devices: 56.8 us -> none  [local(): lax.psum(summed_grads[:, head_width:3 * head_width].astype(jnp.bfloat16),...]
    ppermute x0 -> x25, starting transfers between devices: none -> 36.7 us  [the longest x15 26.3 us: shift_x(): return lax.ppermute(value, 'x', [(i, (i + by) % NX) for i in range(NX)])]
    dot_general x10 -> x13, matrix products: 20.4 us -> 4.18 us  [dot(): lax.dot_general(a, b, (((ca,), (cb,)), ((), ())), preferred_element_type=...]
    all_to_all x0 -> x1, waiting for transfers between devices: none -> 15.6 us  [local(): lax.all_to_all(jnp.broadcast_to(gain_term.reshape(1, 16, 128), (64, 16, 1...]
  transfers between devices with their start and end apart: 8 -> 28, of which waited for: 8 -> 20; matrix products, arithmetic and copies ran while one was open for 2% -> 5% of each run, Pallas kernels for 0% -> 0%
where the time goes in v1:
time: 225 us; the launch traced here: 221 us
  waiting for transfers between devices  100 us (44%)
  starting transfers between devices  44.1 us (20%)
  blocking collectives  27.3 us (12%)
  other arithmetic  15.5 us (7%)
  between operations  15 us (7%)
  local copies, waits for them, and re-layouts  14.7 us (7%)
  matrix products  4.18 us (2%)
    ppermute x15, waiting for transfers between devices, shift_x(): return lax.ppermute(value, 'x', [(i, (i + by) % NX) for i in range(NX)])  34 us
    ppermute x15, starting transfers between devices, shift_x(): return lax.ppermute(value, 'x', [(i, (i + by) % NX) for i in range(NX)])  26.3 us
    ppermute x6, waiting for transfers between devices, swap(): return lax.ppermute(value, axis, [(0, 1), (1, 0)])  21.3 us
    all_gather x1, waiting for transfers between devices, local(): gathered = lax.all_gather(both, 'z')  20.7 us
    all_to_all x1, waiting for transfers between devices, local(): lax.all_to_all(jnp.broadcast_to(gain_term.reshape(1, 16, 128), (64, 16, 1...  15.6 us
    psum x1, blocking collectives, local(): inv_rms = lax.rsqrt(lax.psum(square_sum, TP) / width + 1e-05)  11.9 us
    concatenate x1, other arithmetic, local(): jnp.concatenate([g_q, g_o, g_k, g_v], axis=3)  9.14 us
    all_gather x1, blocking collectives, local(): lax.all_gather(summed_grads[2 * HD:].reshape(2, piece, HD), TP)  8.99 us
  transfers between devices with their start and end apart: 28, of which 20 were waited for; matrix products, arithmetic and copies ran while one was open for 5% of the time, Pallas kernels for 0%

profile of v1, /device:TPU:8, one launch (start us, length us, event | category | flops | bytes accessed | tf_op | source)
XLA Modules:
  0.0 221.0 jit_solution(3554838367439604148)
XLA Ops:
  8.8 3.5 %collective-permute-start.3 = (bf16[320,128]{1,0:T(8,128)(2,1)S(1)}, bf16[320,128]{1,0:T(8,128)(2,1)S(1)}, u32[]{:S(2)}, u32[]{:S(2)}) collective-permute-start(bf16[320,128]{1,0:T(8,128)(2,1)S(1)} %pad_maximum_fusion.14), channel_id=1, source_target_pairs={{0,0},{1,16},{2,128},{3,144},{4,4},{5,20},{6,132},{7,148},{8,8},{9... | collective-permute-start | bytes 245768 | tf_op jit(solution)/shard_map/ppermute | solution.py:88
  12.4 2.7 %collective-permute-done.3 = bf16[320,128]{1,0:T(8,128)(2,1)S(1)} collective-permute-done((bf16[320,128]{1,0:T(8,128)(2,1)S(1)}, bf16[320,128]{1,0:T(8,128)(2,1)S(1)}, u32[]{:S(2)}, u32[]{:S(2)}) %collective-permute-start.3) | collective-permute-done | bytes 81952 | tf_op jit(solution)/shard_map/ppermute | solution.py:88
  15.1 3.2 %collective-permute-done.4 = bf16[320,128]{1,0:T(8,128)(2,1)S(1)} collective-permute-done((bf16[320,128]{1,0:T(8,128)(2,1)S(1)}, bf16[320,128]{1,0:T(8,128)(2,1)S(1)}, u32[]{:S(2)}, u32[]{:S(2)}) %collective-permute-start.4) | collective-permute-done | bytes 81952 | tf_op jit(solution)/shard_map/ppermute | solution.py:89
  19.2 9.8 %collective-permute-start.7 = (bf16[128,512]{1,0:T(8,128)(2,1)S(1)}, bf16[128,512]{1,0:T(8,128)(2,1)S(1)}, u32[]{:S(2)}, u32[]{:S(2)}) collective-permute-start(bf16[128,512]{1,0:T(8,128)(2,1)S(1)} %get-tuple-element.41), channel_id=1, source_target_pairs={{0,96},{32,0},{64,32},{96,64},{1,97},{33,1},{65,33},{97,65},{2,98}... | collective-permute-start | bytes 393224 | tf_op jit(solution)/shard_map/ppermute | solution.py:40
  30.1 11.9 %psum.14 = f32[128,1]{0,1:T(1,128)S(1)} all-reduce(f32[128,1]{0,1:T(1,128)S(1)} %bitcast.114), channel_id=1, replica_groups=mesh['yh'=2,'x'=4,'z'=8,'yl'=2,'c'=2] {'yl','c'}, use_global_device_ids=true, to_apply=%region_1.2 | all-reduce | flops 128 | bytes 1024 | tf_op jit(solution)/shard_map/psum | solution.py:98
  42.3 3.0 %collective-permute-start.2 = (bf16[128,512]{1,0:T(8,128)(2,1)S(1)}, bf16[128,512]{1,0:T(8,128)(2,1)S(1)}, u32[]{:S(2)}, u32[]{:S(2)}) collective-permute-start(bf16[128,512]{1,0:T(8,128)(2,1)S(1)} %get-tuple-element.36), channel_id=1, source_target_pairs={{0,96},{32,0},{64,32},{96,64},{1,97},{33,1},{65,33},{97,65},{2,98}... | collective-permute-start | bytes 393224 | tf_op jit(solution)/shard_map/ppermute | solution.py:40
  45.4 20.7 %all-gather.3.cloned.1.call-done = bf16[16,320,128]{2,1,0:T(8,128)(2,1)} async-done(((bf16[2,320,128]{2,1,0:T(8,128)(2,1)}), bf16[16,320,128]{2,1,0:T(8,128)(2,1)}) %all-gather.3.cloned.1.call-update) | async-done | bytes 1310736 | tf_op jit(solution)/shard_map/all_gather | solution.py:93
  67.1 1.4 dynamic-slice_bitcast_fusion.1
  70.9 4.5 %collective-permute-done = bf16[128,512]{1,0:T(8,128)(2,1)S(1)} collective-permute-done((bf16[128,512]{1,0:T(8,128)(2,1)S(1)}, bf16[128,512]{1,0:T(8,128)(2,1)S(1)}, u32[]{:S(2)}, u32[]{:S(2)}) %collective-permute-start) | collective-permute-done | bytes 131104 | tf_op jit(solution)/shard_map/ppermute | solution.py:40
  77.4 1.6 collective-permute-done.8
  80.3 2.9 %collective-permute-start.10 = (f32[128,640]{0,1:T(8,128)}, f32[128,640]{0,1:T(8,128)S(1)}, u32[]{:S(2)}, u32[]{:S(2)}) collective-permute-start(f32[128,640]{0,1:T(8,128)} %get-tuple-element.12), channel_id=1, source_target_pairs={{0,64},{32,96},{64,0},{96,32},{1,65},{33,97},{65,1},{97,33},{2,66}... | collective-permute-start | bytes 983048 | tf_op jit(solution)/shard_map/ppermute | solution.py:40
  83.2 1.4 collective-permute-start.9
  84.6 13.9 %collective-permute-done.11 = f32[128,640]{0,1:T(8,128)S(1)} collective-permute-done((f32[128,640]{0,1:T(8,128)}, f32[128,640]{0,1:T(8,128)S(1)}, u32[]{:S(2)}, u32[]{:S(2)}) %collective-permute-start.11) | collective-permute-done | bytes 327712 | tf_op jit(solution)/shard_map/ppermute | solution.py:40
  100.1 5.3 %collective-permute-done.12 = f32[128,384]{0,1:T(8,128)S(1)} collective-permute-done((f32[128,384]{0,1:T(8,128)S(1)}, f32[128,384]{0,1:T(8,128)S(1)}, u32[]{:S(2)}, u32[]{:S(2)}) %collective-permute-start.12) | collective-permute-done | bytes 196640 | tf_op jit(solution)/shard_map/ppermute | solution.py:44
  108.9 3.7 %collective-permute-start.17 = (bf16[128,384]{0,1:T(8,128)(2,1)S(1)}, bf16[128,384]{0,1:T(8,128)(2,1)S(1)}, u32[]{:S(2)}, u32[]{:S(2)}) collective-permute-start(bf16[128,384]{0,1:T(8,128)(2,1)S(1)} %pad_maximum_fusion.13), channel_id=1, source_target_pairs={{0,96},{32,0},{64,32},{96,64},{1,97},{33,1},{65,33},{97,65},{2,98}... | collective-permute-start | bytes 294920 | tf_op jit(solution)/shard_map/ppermute | solution.py:40
  113.5 3.5 %collective-permute-done.17 = bf16[128,384]{0,1:T(8,128)(2,1)S(1)} collective-permute-done((bf16[128,384]{0,1:T(8,128)(2,1)S(1)}, bf16[128,384]{0,1:T(8,128)(2,1)S(1)}, u32[]{:S(2)}, u32[]{:S(2)}) %collective-permute-start.17) | collective-permute-done | bytes 98336 | tf_op jit(solution)/shard_map/ppermute | solution.py:40
  117.0 2.7 %collective-permute-done.16 = bf16[128,384]{0,1:T(8,128)(2,1)S(1)} collective-permute-done((bf16[128,384]{0,1:T(8,128)(2,1)S(1)}, bf16[128,384]{0,1:T(8,128)(2,1)S(1)}, u32[]{:S(2)}, u32[]{:S(2)}) %collective-permute-start.16) | collective-permute-done | bytes 98336 | tf_op jit(solution)/shard_map/ppermute | solution.py:40
  121.3 10.4 %collective-permute-done.18 = bf16[512,384]{0,1:T(8,128)(2,1)S(1)} collective-permute-done((bf16[512,384]{0,1:T(8,128)(2,1)S(1)}, bf16[512,384]{0,1:T(8,128)(2,1)S(1)}, u32[]{:S(2)}, u32[]{:S(2)}) %collective-permute-start.18) | collective-permute-done | bytes 393248 | tf_op jit(solution)/shard_map/ppermute | solution.py:44
  132.1 2.1 collective-permute-done.19
  139.2 9.1 %pad_maximum_fusion.1 = bf16[2,4,2,320,128]{4,2,0,3,1:T(2,128)(2,1)S(1)} fusion(bf16[2,4,2,32,128]{4,2,0,3,1:T(2,128)(2,1)S(1)} %copy.59, bf16[2,4,2,32,128]{4,2,0,3,1:T(2,128)(2,1)S(1)} %copy.58, bf16[2,4,2,128,128]{4,2,0,3,1:T(2,128)(2,1)S(1)} %bitcast.93, bf16[2,4,2,128,128]{4,2,0,3,1:T(2,128)(2,1)S(1)} %bitcast.94), kind=kLoop, calls=%fused_computation.10 | loop fusion | flops 1966080 | bytes 2621440 | tf_op jit(solution)/shard_map/concatenate | solution.py:169
  148.4 1.3 copy.60
  153.1 1.7 collective-permute-start.22
  154.8 4.3 %collective-permute-done.20 = bf16[128,512]{1,0:T(8,128)(2,1)S(1)} collective-permute-done((bf16[128,512]{1,0:T(8,128)(2,1)S(1)}, bf16[128,512]{1,0:T(8,128)(2,1)S(1)}, u32[]{:S(2)}, u32[]{:S(2)}) %collective-permute-start.20) | collective-permute-done | bytes 131104 | tf_op jit(solution)/shard_map/ppermute | solution.py:40
  159.1 1.6 collective-permute-done.21
  160.7 2.0 collective-permute-done.22
  164.0 7.3 %all-to-all-start = ((f32[64,16,128]{2,1,0:T(8,128)}), f32[64,16,128]{2,1,0:T(8,128)S(1)}, u32[]{:S(2)}, u32[]{:S(2)}) async-start(f32[64,16,128]{2,1,0:T(8,128)} %broadcast_in_dim.32), calls=%async_computation | async-start | bytes 1048576 | tf_op jit(solution)/shard_map/all_to_all | solution.py:194
  171.3 6.4 %psum.15 = f32[128,1]{0,1:T(1,128)S(1)} all-reduce(f32[128,1]{0,1:T(1,128)S(1)} %bitcast.113), channel_id=1, replica_groups=mesh['yh'=2,'x'=4,'z'=8,'yl'=2,'c'=2] {'yl','c'}, use_global_device_ids=true, to_apply=%region_6.7 | all-reduce | flops 128 | bytes 1024 | tf_op jit(solution)/shard_map/psum | solution.py:191
  179.0 15.6 %all-to-all-done = f32[64,16,128]{2,1,0:T(8,128)S(1)} async-done(((f32[64,16,128]{2,1,0:T(8,128)}), f32[64,16,128]{2,1,0:T(8,128)S(1)}, u32[]{:S(2)}, u32[]{:S(2)}) %all-to-all-start) | async-done | bytes 524320 | tf_op jit(solution)/shard_map/all_to_all | solution.py:194
  195.7 1.8 collective-permute-start.24
  197.5 3.0 %collective-permute-start.23 = (bf16[320,128]{1,0:T(8,128)(2,1)S(1)}, bf16[320,128]{1,0:T(8,128)(2,1)S(1)}, u32[]{:S(2)}, u32[]{:S(2)}) collective-permute-start(bf16[320,128]{1,0:T(8,128)(2,1)S(1)} %get-tuple-element.54), channel_id=1, source_target_pairs={{0,0},{16,1},{128,2},{144,3},{4,4},{20,5},{132,6},{148,7},{8,8},{2... | collective-permute-start | bytes 245768 | tf_op jit(solution)/shard_map/ppermute | solution.py:173
  201.2 2.7 %collective-permute-done.23 = bf16[320,128]{1,0:T(8,128)(2,1)S(1)} collective-permute-done((bf16[320,128]{1,0:T(8,128)(2,1)S(1)}, bf16[320,128]{1,0:T(8,128)(2,1)S(1)}, u32[]{:S(2)}, u32[]{:S(2)}) %collective-permute-start.23) | collective-permute-done | bytes 81952 | tf_op jit(solution)/shard_map/ppermute | solution.py:173
  204.5 9.0 %all_gather.11 = f32[4,2,32,128]{3,2,1,0:T(8,128)S(1)} all-gather(f32[1,2,32,128]{3,2,1,0:T(8,128)S(1)} %bitcast.109), channel_id=1, replica_groups=mesh['yh'=2,'x'=4,'z'=8,'yl'=2,'c'=2] {'yl','c'}, dimensions={0}, use_global_device_ids=true | all-gather | bytes 163840 | tf_op jit(solution)/shard_map/all_gather | solution.py:177
  (165 shorter events, 32.0 us)
Async XLA Ops:
  7.2 22.8 %copy-start.9 = (bf16[2048]{0:T(1024)(128)(2,1)S(1)}, bf16[2048]{0:T(1024)(128)(2,1)}, u32[]{:S(2)}) copy-start(bf16[2048]{0:T(1024)(128)(2,1)} %param.8) | copy-start | bytes 12292
  7.2 22.8 %copy-start = (bf16[128,2048]{1,0:T(8,128)(2,1)S(1)}, bf16[128,2048]{1,0:T(8,128)(2,1)}, u32[]{:S(2)}) copy-start(bf16[128,2048]{1,0:T(8,128)(2,1)} %param.7) | copy-start | bytes 1572868
  7.2 58.9 %all-gather.3.cloned.1.call-start = ((), (), s32[]{:S(2)}) async-start(), calls=%async_computation.3 | async-start | bytes 1474560 | tf_op jit(solution)/shard_map/all_gather | solution.py:93
  8.8 6.3 %collective-permute-start.3 = (bf16[320,128]{1,0:T(8,128)(2,1)S(1)}, bf16[320,128]{1,0:T(8,128)(2,1)S(1)}, u32[]{:S(2)}, u32[]{:S(2)}) collective-permute-start(bf16[320,128]{1,0:T(8,128)(2,1)S(1)} %pad_maximum_fusion.14), channel_id=1, source_target_pairs={{0,0},{1,16},{2,128},{3,144},{4,4},{5,20},{6,132},{7,148},{8,8},{9... | collective-permute-start | bytes 245768 | tf_op jit(solution)/shard_map/ppermute | solution.py:88
  12.3 6.0 %collective-permute-start.4 = (bf16[320,128]{1,0:T(8,128)(2,1)S(1)}, bf16[320,128]{1,0:T(8,128)(2,1)S(1)}, u32[]{:S(2)}, u32[]{:S(2)}) collective-permute-start(bf16[320,128]{1,0:T(8,128)(2,1)S(1)} %pad_maximum_fusion.14), channel_id=1, source_target_pairs={{0,128},{1,144},{2,0},{3,16},{4,132},{5,148},{6,4},{7,20},{8,136},... | collective-permute-start | bytes 245768 | tf_op jit(solution)/shard_map/ppermute | solution.py:89
  19.1 175.7 %reduce-scatter.2.cloned.1.call-start = ((), (), s32[]{:S(2)}) async-start(), calls=%async_computation.2 | async-start | bytes 1474560 | tf_op jit(solution)/shard_map/reduce_scatter | solution.py:170
  19.2 57.8 %copy-start.5 = (bf16[128,512]{1,0:T(8,128)(2,1)}, bf16[128,512]{1,0:T(8,128)(2,1)S(1)}, u32[]{:S(2)}) copy-start(bf16[128,512]{1,0:T(8,128)(2,1)S(1)} %get-tuple-element.39) | copy-start | bytes 393220
  19.2 49.8 %collective-permute-start.7 = (bf16[128,512]{1,0:T(8,128)(2,1)S(1)}, bf16[128,512]{1,0:T(8,128)(2,1)S(1)}, u32[]{:S(2)}, u32[]{:S(2)}) collective-permute-start(bf16[128,512]{1,0:T(8,128)(2,1)S(1)} %get-tuple-element.41), channel_id=1, source_target_pairs={{0,96},{32,0},{64,32},{96,64},{1,97},{33,1},{65,33},{97,65},{2,98}... | collective-permute-start | bytes 393224 | tf_op jit(solution)/shard_map/ppermute | solution.py:40
  29.0 41.4 %collective-permute-start.6 = (bf16[128,512]{1,0:T(8,128)(2,1)S(1)}, bf16[128,512]{1,0:T(8,128)(2,1)S(1)}, u32[]{:S(2)}, u32[]{:S(2)}) collective-permute-start(bf16[128,512]{1,0:T(8,128)(2,1)S(1)} %get-tuple-element.42), channel_id=1, source_target_pairs={{0,64},{32,96},{64,0},{96,32},{1,65},{33,97},{65,1},{97,33},{2,66}... | collective-permute-start | bytes 393224 | tf_op jit(solution)/shard_map/ppermute | solution.py:40
  29.5 40.9 %collective-permute-start.5 = (bf16[128,512]{1,0:T(8,128)(2,1)S(1)}, bf16[128,512]{1,0:T(8,128)(2,1)S(1)}, u32[]{:S(2)}, u32[]{:S(2)}) collective-permute-start(bf16[128,512]{1,0:T(8,128)(2,1)S(1)} %get-tuple-element.40), channel_id=1, source_target_pairs={{0,32},{32,64},{64,96},{96,0},{1,33},{33,65},{65,97},{97,1},{2,34}... | collective-permute-start | bytes 393224 | tf_op jit(solution)/shard_map/ppermute | solution.py:40
  42.3 34.2 %copy-start.7 = (bf16[128,512]{1,0:T(8,128)(2,1)}, bf16[128,512]{1,0:T(8,128)(2,1)S(1)}, u32[]{:S(2)}) copy-start(bf16[128,512]{1,0:T(8,128)(2,1)S(1)} %get-tuple-element.35) | copy-start | bytes 393220
  42.3 28.5 %collective-permute-start.2 = (bf16[128,512]{1,0:T(8,128)(2,1)S(1)}, bf16[128,512]{1,0:T(8,128)(2,1)S(1)}, u32[]{:S(2)}, u32[]{:S(2)}) collective-permute-start(bf16[128,512]{1,0:T(8,128)(2,1)S(1)} %get-tuple-element.36), channel_id=1, source_target_pairs={{0,96},{32,0},{64,32},{96,64},{1,97},{33,1},{65,33},{97,65},{2,98}... | collective-permute-start | bytes 393224 | tf_op jit(solution)/shard_map/ppermute | solution.py:40
  45.4 25.5 %collective-permute-start.1 = (bf16[128,512]{1,0:T(8,128)(2,1)S(1)}, bf16[128,512]{1,0:T(8,128)(2,1)S(1)}, u32[]{:S(2)}, u32[]{:S(2)}) collective-permute-start(bf16[128,512]{1,0:T(8,128)(2,1)S(1)} %get-tuple-element.37), channel_id=1, source_target_pairs={{0,64},{32,96},{64,0},{96,32},{1,65},{33,97},{65,1},{97,33},{2,66}... | collective-permute-start | bytes 393224 | tf_op jit(solution)/shard_map/ppermute | solution.py:40
  69.1 6.3 %collective-permute-start = (bf16[128,512]{1,0:T(8,128)(2,1)S(1)}, bf16[128,512]{1,0:T(8,128)(2,1)S(1)}, u32[]{:S(2)}, u32[]{:S(2)}) collective-permute-start(bf16[128,512]{1,0:T(8,128)(2,1)S(1)} %get-tuple-element.38), channel_id=1, source_target_pairs={{0,32},{32,64},{64,96},{96,0},{1,33},{33,65},{65,97},{97,1},{2,34}... | collective-permute-start | bytes 393224 | tf_op jit(solution)/shard_map/ppermute | solution.py:40
  75.9 3.1 %collective-permute-start.8 = (f32[512,640]{0,1:T(8,128)S(1)}, f32[512,640]{0,1:T(8,128)S(1)}, u32[]{:S(2)}, u32[]{:S(2)}) collective-permute-start(f32[512,640]{0,1:T(8,128)S(1)} %pad_maximum_fusion), channel_id=1, source_target_pairs={{0,1},{1,0},{2,3},{3,2},{4,5},{5,4},{6,7},{7,6},{8,9},{9,8},{10,11... | collective-permute-start | bytes 3932168 | tf_op jit(solution)/shard_map/ppermute | solution.py:44
  80.3 18.2 %collective-permute-start.11 = (f32[128,640]{0,1:T(8,128)}, f32[128,640]{0,1:T(8,128)S(1)}, u32[]{:S(2)}, u32[]{:S(2)}) collective-permute-start(f32[128,640]{0,1:T(8,128)} %get-tuple-element.11), channel_id=1, source_target_pairs={{0,32},{32,64},{64,96},{96,0},{1,33},{33,65},{65,97},{97,1},{2,34}... | collective-permute-start | bytes 983048 | tf_op jit(solution)/shard_map/ppermute | solution.py:40
  80.3 18.2 %collective-permute-start.10 = (f32[128,640]{0,1:T(8,128)}, f32[128,640]{0,1:T(8,128)S(1)}, u32[]{:S(2)}, u32[]{:S(2)}) collective-permute-start(f32[128,640]{0,1:T(8,128)} %get-tuple-element.12), channel_id=1, source_target_pairs={{0,64},{32,96},{64,0},{96,32},{1,65},{33,97},{65,1},{97,33},{2,66}... | collective-permute-start | bytes 983048 | tf_op jit(solution)/shard_map/ppermute | solution.py:40
  83.2 15.9 %collective-permute-start.9 = (f32[128,640]{0,1:T(8,128)}, f32[128,640]{0,1:T(8,128)S(1)}, u32[]{:S(2)}, u32[]{:S(2)}) collective-permute-start(f32[128,640]{0,1:T(8,128)} %get-tuple-element.10), channel_id=1, source_target_pairs={{0,96},{32,0},{64,32},{96,64},{1,97},{33,1},{65,33},{97,65},{2,98}... | collective-permute-start | bytes 983048 | tf_op jit(solution)/shard_map/ppermute | solution.py:40
  99.3 6.1 %collective-permute-start.12 = (f32[128,384]{0,1:T(8,128)S(1)}, f32[128,384]{0,1:T(8,128)S(1)}, u32[]{:S(2)}, u32[]{:S(2)}) collective-permute-start(f32[128,384]{0,1:T(8,128)S(1)} %pad_maximum_fusion.6), channel_id=1, source_target_pairs={{0,2},{2,0},{1,3},{3,1},{4,6},{6,4},{5,7},{7,5},{8,10},{10,8},{9,1... | collective-permute-start | bytes 589832 | tf_op jit(solution)/shard_map/ppermute | solution.py:44
  105.4 1.3 collective-permute-start.13
  107.6 1.3 collective-permute-start.14
  108.9 8.2 %collective-permute-start.17 = (bf16[128,384]{0,1:T(8,128)(2,1)S(1)}, bf16[128,384]{0,1:T(8,128)(2,1)S(1)}, u32[]{:S(2)}, u32[]{:S(2)}) collective-permute-start(bf16[128,384]{0,1:T(8,128)(2,1)S(1)} %pad_maximum_fusion.13), channel_id=1, source_target_pairs={{0,96},{32,0},{64,32},{96,64},{1,97},{33,1},{65,33},{97,65},{2,98}... | collective-permute-start | bytes 294920 | tf_op jit(solution)/shard_map/ppermute | solution.py:40
  112.6 7.2 %collective-permute-start.16 = (bf16[128,384]{0,1:T(8,128)(2,1)S(1)}, bf16[128,384]{0,1:T(8,128)(2,1)S(1)}, u32[]{:S(2)}, u32[]{:S(2)}) collective-permute-start(bf16[128,384]{0,1:T(8,128)(2,1)S(1)} %pad_maximum_fusion.13), channel_id=1, source_target_pairs={{0,64},{32,96},{64,0},{96,32},{1,65},{33,97},{65,1},{97,33},{2,66}... | collective-permute-start | bytes 294920 | tf_op jit(solution)/shard_map/ppermute | solution.py:40
  113.0 7.6 %collective-permute-start.15 = (bf16[128,384]{0,1:T(8,128)(2,1)S(1)}, bf16[128,384]{0,1:T(8,128)(2,1)S(1)}, u32[]{:S(2)}, u32[]{:S(2)}) collective-permute-start(bf16[128,384]{0,1:T(8,128)(2,1)S(1)} %pad_maximum_fusion.13), channel_id=1, source_target_pairs={{0,32},{32,64},{64,96},{96,0},{1,33},{33,65},{65,97},{97,1},{2,34}... | collective-permute-start | bytes 294920 | tf_op jit(solution)/shard_map/ppermute | solution.py:40
  120.7 11.0 %collective-permute-start.18 = (bf16[512,384]{0,1:T(8,128)(2,1)S(1)}, bf16[512,384]{0,1:T(8,128)(2,1)S(1)}, u32[]{:S(2)}, u32[]{:S(2)}) collective-permute-start(bf16[512,384]{0,1:T(8,128)(2,1)S(1)} %pad_maximum_fusion.5), channel_id=1, source_target_pairs={{0,2},{2,0},{1,3},{3,1},{4,6},{6,4},{5,7},{7,5},{8,10},{10,8},{9,1... | collective-permute-start | bytes 1179656 | tf_op jit(solution)/shard_map/ppermute | solution.py:44
  132.0 2.2 collective-permute-start.19
  152.5 6.6 %collective-permute-start.20 = (bf16[128,512]{1,0:T(8,128)(2,1)S(1)}, bf16[128,512]{1,0:T(8,128)(2,1)S(1)}, u32[]{:S(2)}, u32[]{:S(2)}) collective-permute-start(bf16[128,512]{1,0:T(8,128)(2,1)S(1)} %get-tuple-element.33), channel_id=1, source_target_pairs={{0,96},{32,0},{64,32},{96,64},{1,97},{33,1},{65,33},{97,65},{2,98}... | collective-permute-start | bytes 393224 | tf_op jit(solution)/shard_map/ppermute | solution.py:40
  152.8 7.9 %collective-permute-start.21 = (bf16[128,512]{1,0:T(8,128)(2,1)S(1)}, bf16[128,512]{1,0:T(8,128)(2,1)S(1)}, u32[]{:S(2)}, u32[]{:S(2)}) collective-permute-start(bf16[128,512]{1,0:T(8,128)(2,1)S(1)} %get-tuple-element.32), channel_id=1, source_target_pairs={{0,64},{32,96},{64,0},{96,32},{1,65},{33,97},{65,1},{97,33},{2,66}... | collective-permute-start | bytes 393224 | tf_op jit(solution)/shard_map/ppermute | solution.py:40
  153.1 9.6 %collective-permute-start.22 = (bf16[128,512]{1,0:T(8,128)(2,1)S(1)}, bf16[128,512]{1,0:T(8,128)(2,1)S(1)}, u32[]{:S(2)}, u32[]{:S(2)}) collective-permute-start(bf16[128,512]{1,0:T(8,128)(2,1)S(1)} %get-tuple-element.31), channel_id=1, source_target_pairs={{0,32},{32,64},{64,96},{96,0},{1,33},{33,65},{65,97},{97,1},{2,34}... | collective-permute-start | bytes 393224 | tf_op jit(solution)/shard_map/ppermute | solution.py:40
  164.0 30.7 %all-to-all-start = ((f32[64,16,128]{2,1,0:T(8,128)}), f32[64,16,128]{2,1,0:T(8,128)S(1)}, u32[]{:S(2)}, u32[]{:S(2)}) async-start(f32[64,16,128]{2,1,0:T(8,128)} %broadcast_in_dim.32), calls=%async_computation | async-start | bytes 1048576 | tf_op jit(solution)/shard_map/all_to_all | solution.py:194
  195.7 5.4 %collective-permute-start.24 = (bf16[320,128]{1,0:T(8,128)(2,1)S(1)}, bf16[320,128]{1,0:T(8,128)(2,1)S(1)}, u32[]{:S(2)}, u32[]{:S(2)}) collective-permute-start(bf16[320,128]{1,0:T(8,128)(2,1)S(1)} %get-tuple-element.55), channel_id=1, source_target_pairs={{128,0},{144,1},{0,2},{16,3},{132,4},{148,5},{4,6},{20,7},{136,8},... | collective-permute-start | bytes 245768 | tf_op jit(solution)/shard_map/ppermute | solution.py:174
  197.5 6.3 %collective-permute-start.23 = (bf16[320,128]{1,0:T(8,128)(2,1)S(1)}, bf16[320,128]{1,0:T(8,128)(2,1)S(1)}, u32[]{:S(2)}, u32[]{:S(2)}) collective-permute-start(bf16[320,128]{1,0:T(8,128)(2,1)S(1)} %get-tuple-element.54), channel_id=1, source_target_pairs={{0,0},{16,1},{128,2},{144,3},{4,4},{20,5},{132,6},{148,7},{8,8},{2... | collective-permute-start | bytes 245768 | tf_op jit(solution)/shard_map/ppermute | solution.py:173
  (19 other events, 60.3 us)
Sparse Core Ops, SparseCore 0:
  19.2 46.8 all-gather.2
  149.9 41.4 reduce-scatter.1
